TPU v7x, 128 devices: a whole 4x4x4 slice. The times are simulated.
128 devices in a mesh: dp: 8 (over z, core), ctx: 16 (over y, x).
Axes of the slice: x: 4, y: 4, z: 4, core: 2. Of those that a mesh axis runs over, the one named last changes fastest.
Arguments:
- tokens: bfloat16 [24576, 1024], P(('dp', 'ctx')), may hold values from -55 to 55
- segments: int32 [8, 3072], P('dp', 'ctx'), may hold values from 0 to 7, never falling along the last dimension, each value on 1 to 1536 neighbouring positions
- w_in: bfloat16 [1024, 4096], replicated, may hold values from -0.1875 to 0.1875
- w_out: bfloat16 [1024, 1024], replicated, may hold values from -0.1875 to 0.1875
- grad_out: bfloat16 [24576, 1024], P(('dp', 'ctx')), may hold values from -24 to 24
Outputs:
- layer_out: bfloat16 [24576, 1024], P(('dp', 'ctx'))
- grad_tokens: bfloat16 [24576, 1024], P(('dp', 'ctx'))
- out_grad: float32 [1024, 1024], P(('dp', 'ctx'))
Inputs may be any that keep to these rules, and one draw needn't show every extreme that they name: `segments`: along each stream's stored rows the history number never falls; each of the 8 histories holds 1 to 1536 events, one exactly 1536.
All inputs are finite; a program needn't handle non-finite values.
Results may differ from a plain program's by a relative error of at most 0.008.
Values may be sent and summed in bfloat16 or wider, within the bound.
A program may use at most 128 MiB of HBM per device.

v0:
```python
import jax
import jax.numpy as jnp
from jax import lax
from jax.sharding import PartitionSpec as P

HEADS = 8
EPS = 1e-05


def silu_grad(value):
    sigmoid_v = jax.nn.sigmoid(value)
    return sigmoid_v * (1.0 + value * (1.0 - sigmoid_v))


def norm_rows(matrix):
    average = jnp.mean(matrix, axis=-1, keepdims=True)
    centred = matrix - average
    inverse = lax.rsqrt(jnp.mean(centred * centred, axis=-1, keepdims=True) + EPS)
    return (centred * inverse, inverse)


def norm_back(gradient, normed, inverse):
    first = jnp.mean(gradient, axis=-1, keepdims=True)
    second = jnp.mean(gradient * normed, axis=-1, keepdims=True)
    return (gradient - first - normed * second) * inverse


def head_major(matrix):
    return matrix.reshape(matrix.shape[0], HEADS, matrix.shape[1] // HEADS).transpose(1, 0, 2)


def row_major(stacked):
    return stacked.transpose(1, 0, 2).reshape(stacked.shape[1], stacked.shape[0] * stacked.shape[2])


def place_of(stored, own_rows, ctx_count):
    block = stored // own_rows
    inner = stored % own_rows
    half = own_rows // 2
    return jnp.where(
        inner < half, block * half + inner, (2 * ctx_count - 1 - block) * half + inner - half
    )


def on_device(tokens, segments, w_in, w_out, grad_out):
    own_rows, model_width = tokens.shape
    ctx_count = lax.axis_size("ctx")
    score_scale = (model_width // HEADS) ** (-0.5)
    device_pos = lax.axis_index("ctx")
    positions = place_of(
        device_pos * own_rows + jnp.arange(own_rows, dtype=jnp.int32), own_rows, ctx_count
    )
    history = segments[0]
    xfloat = tokens.astype(jnp.float32)
    normed, inv_x = norm_rows(xfloat)
    normed_b = normed.astype(jnp.bfloat16)
    preact = jnp.dot(normed_b, w_in, preferred_element_type=jnp.float32)
    act = jax.nn.silu(preact).astype(jnp.bfloat16)
    gate_u = act[:, :model_width]
    own_values = act[:, model_width : 2 * model_width]
    queries = act[:, 2 * model_width : 3 * model_width]
    own_keys = act[:, 3 * model_width :]
    keys_all, values_all, history_all = (
        lax.all_gather(own_keys, "ctx", axis=0, tiled=True),
        lax.all_gather(own_values, "ctx", axis=0, tiled=True),
        lax.all_gather(history, "ctx", axis=0, tiled=True),
    )
    places_all = place_of(jnp.arange(keys_all.shape[0], dtype=jnp.int32), own_rows, ctx_count)
    visible = (history[:, None] == history_all[None, :]) & (
        positions[:, None] >= places_all[None, :]
    )
    query_h = head_major(queries)
    keys_h = head_major(keys_all)
    values_h = head_major(values_all)

    def forward_head(operands):
        one_q, one_k, one_v = operands
        scores = jnp.dot(one_q, one_k.T, preferred_element_type=jnp.float32) * score_scale
        weights = jnp.where(visible, jax.nn.silu(scores), 0.0).astype(jnp.bfloat16)
        return jnp.dot(weights, one_v, preferred_element_type=jnp.float32)

    mixed = row_major(lax.map(forward_head, (query_h, keys_h, values_h)))
    mixed_n, inv_o = norm_rows(mixed)
    gated = (mixed_n * gate_u.astype(jnp.float32)).astype(jnp.bfloat16)
    layer_out = (jnp.dot(gated, w_out, preferred_element_type=jnp.float32) + xfloat).astype(
        jnp.bfloat16
    )
    total_rows = own_rows * lax.axis_size(("dp", "ctx"))
    out_grad = lax.psum_scatter(
        jnp.einsum("re,rd->ed", grad_out, gated, preferred_element_type=jnp.float32),
        ("dp", "ctx"),
        scatter_dimension=0,
        tiled=True,
    ) * total_rows ** (-0.5)
    grad_gated = jnp.einsum("re,de->rd", grad_out, w_out, preferred_element_type=jnp.float32)
    grad_u = grad_gated * mixed_n
    grad_norm = grad_gated * gate_u.astype(jnp.float32)
    grad_mixed = norm_back(grad_norm, mixed_n, inv_o).astype(jnp.bfloat16)
    grad_h = head_major(grad_mixed)

    def query_head(operands):
        one_q, one_k, one_v, one_g = operands
        scores = jnp.dot(one_q, one_k.T, preferred_element_type=jnp.float32) * score_scale
        grad_weights = jnp.dot(one_g, one_v.T, preferred_element_type=jnp.float32)
        grad_scores = (
            jnp.where(visible, grad_weights * silu_grad(scores), 0.0) * score_scale
        ).astype(jnp.bfloat16)
        return jnp.dot(grad_scores, one_k, preferred_element_type=jnp.float32)

    grad_queries = row_major(lax.map(query_head, (query_h, keys_h, values_h, grad_h)))
    own_keys_h = head_major(own_keys)
    own_values_h = head_major(own_values)
    piece_q = lax.all_gather(queries, "ctx", axis=0, tiled=True)
    piece_grad = lax.all_gather(grad_mixed, "ctx", axis=0, tiled=True)
    piece_hist = lax.all_gather(history, "ctx", axis=0, tiled=True)
    row_count = piece_q.shape[0]
    piece_pos = place_of(jnp.arange(row_count, dtype=jnp.int32), own_rows, ctx_count)
    piece_visible = (piece_hist[:, None] == history[None, :]) & (
        piece_pos[:, None] >= positions[None, :]
    )

    def key_head(operands):
        one_q, one_g, one_k, one_v = operands
        scores = jnp.dot(one_q, one_k.T, preferred_element_type=jnp.float32) * score_scale
        weights = jnp.where(piece_visible, jax.nn.silu(scores), 0.0).astype(jnp.bfloat16)
        grad_weights = jnp.dot(one_g, one_v.T, preferred_element_type=jnp.float32)
        grad_scores = (
            jnp.where(piece_visible, grad_weights * silu_grad(scores), 0.0) * score_scale
        ).astype(jnp.bfloat16)
        key_part = jnp.dot(grad_scores.T, one_q, preferred_element_type=jnp.float32)
        value_part = jnp.dot(weights.T, one_g, preferred_element_type=jnp.float32)
        return (key_part, value_part)

    key_part, value_part = lax.map(
        key_head, (head_major(piece_q), head_major(piece_grad), own_keys_h, own_values_h)
    )
    grad_keys = row_major(key_part)
    grad_values = row_major(value_part)
    grad_all = jnp.concatenate([grad_u, grad_values, grad_queries, grad_keys], axis=1)
    grad_pre = (grad_all * silu_grad(preact)).astype(jnp.bfloat16)
    grad_rows = jnp.einsum("rf,df->rd", grad_pre, w_in, preferred_element_type=jnp.float32)
    grad_tokens = (grad_out.astype(jnp.float32) + norm_back(grad_rows, normed, inv_x)).astype(
        jnp.bfloat16
    )
    return (layer_out, grad_tokens, out_grad)


def solution(mesh):
    return jax.shard_map(
        on_device,
        mesh=mesh,
        in_specs=(P(("dp", "ctx"), None), P("dp", "ctx"), P(), P(), P(("dp", "ctx"), None)),
        out_specs=(P(("dp", "ctx"), None), P(("dp", "ctx"), None), P(("dp", "ctx"), None)),
        check_vma=False,
    )
```

profile of v0, /device:TPU:1, one launch (start us, length us, event | category | flops | bytes accessed | tf_op | source)
XLA Modules:
  0.0 1003.1 jit_solution(6318163071438569828)
XLA Ops:
  9.8 7.2 multiply_convert_fusion
  23.6 62.2 %all-reduce = s32[3072]{0:T(1024)S(1)} all-reduce(s32[3072]{0:T(1024)S(1)} %dynamic-update-slice), channel_id=2, replica_groups=mesh['dp'=8,'ctx'=16] {'ctx'}, use_global_device_ids=true, to_apply=%add | all-reduce | flops 3072 | bytes 24576 | tf_op jit(solution)/shard_map/all_gather | solution.py:66
  85.8 6.6 bitcast_bitcast_fusion.2
  92.4 55.4 %all-gather.6.cloned.1.call-done = bf16[3072,1024]{1,0:T(8,128)(2,1)} async-done(((bf16[192,1024]{1,0:T(8,128)(2,1)}), bf16[3072,1024]{1,0:T(8,128)(2,1)}) %all-gather.6.cloned.1.call-update) | async-done | bytes 6291472 | tf_op jit(solution)/shard_map/all_gather | solution.py:64
  147.8 6.5 bitcast_bitcast_fusion.3
  154.4 22.1 %while.35 = (s32[]{:T(128)}, f32[8,192,128]{2,1,0:T(8,128)S(1)}, bf16[8,192,128]{2,1,0:T(8,128)(2,1)}, bf16[8,3072,128]{2,1,0:T(8,128)(2,1)}, bf16[8,3072,128]{2...) while((s32[]{:T(128)}, f32[8,192,128]{2,1,0:T(8,128)S(1)}, ...), condition=%wide.region_3.4_spmd.clone, body=%wide.region_2.3_spmd.clone.sunk | while | flops 307888128 | bytes 1749093 | solution.py:82
  176.8 3.8 convolution_bitcast_fusion
  180.6 5.4 copy.34
  195.5 58.9 %while.37 = (s32[]{:T(128)}, f32[8,192,128]{2,1,0:T(8,128)}, bf16[8,192,128]{2,1,0:T(8,128)(2,1)}, bf16[8,3072,128]{2,1,0:T(8,128)(2,1)}, bf16[8,192,128]{2,1,0:...) while((s32[]{:T(128)}, f32[8,192,128]{2,1,0:T(8,128)}, ...), condition=%wide.region_11.12_spmd.clone, body=%wide.region_10.11_spmd.clone.sunk | while | flops 461832192 | bytes 7303789 | solution.py:110
  198.6 4.4 fusion.202
  206.0 4.3 fusion.202
  213.3 4.3 fusion.202
  220.7 4.3 fusion.202
  228.0 4.3 fusion.202
  235.4 4.3 fusion.202
  242.7 4.3 fusion.202
  250.1 4.3 fusion.202
  258.9 6.6 bitcast_bitcast_fusion
  265.5 559.4 %reduce-scatter.4.cloned.1.call-done = f32[8,1024]{1,0:T(8,128)} async-done(((f32[1024,1024]{1,0:T(8,128)}), f32[8,1024]{1,0:T(8,128)}) %reduce-scatter.4.cloned.1.call-update) | async-done | bytes 32784
  826.6 87.1 %all-gather.10.cloned.1.call-done = bf16[3072,1024]{1,0:T(8,128)(2,1)} async-done(((bf16[192,1024]{1,0:T(8,128)(2,1)}), bf16[3072,1024]{1,0:T(8,128)(2,1)}) %all-gather.10.cloned.1.call-update) | async-done | bytes 6291472 | tf_op jit(solution)/shard_map/all_gather | solution.py:114
  913.7 6.6 bitcast_bitcast_fusion.1
  922.3 63.1 %while.36 = (s32[]{:T(128)}, f32[8,192,128]{2,1,0:T(8,128)}, f32[8,192,128]{2,1,0:T(8,128)}, bf16[8,3072,128]{2,1,0:T(8,128)(2,1)}, bf16[8,192,128]{2,1,0:T(8,12...) while((s32[]{:T(128)}, f32[8,192,128]{2,1,0:T(8,128)}, ...), condition=%wide.region_9.10_spmd.clone, body=%wide.region_8.9_spmd.clone.sunk | while | flops 618135552 | bytes 10574965 | solution.py:134
  939.6 3.6 fusion.195
  988.0 7.4 fusion.148
  (107 shorter events, 135.9 us)
Async XLA Ops:
  7.2 179.0 %copy-start = (bf16[1024,1024]{1,0:T(8,128)(2,1)S(1)}, bf16[1024,1024]{1,0:T(8,128)(2,1)}, u32[]{:S(2)}) copy-start(bf16[1024,1024]{1,0:T(8,128)(2,1)} %param.14) | copy-start | bytes 6291460
  7.2 78.6 %all-gather.8.cloned.1.call-start = ((), (), s32[]{:S(2)}) async-start(), calls=%async_computation.2 | async-start | bytes 6684672 | tf_op jit(solution)/shard_map/all_gather | solution.py:65
  16.9 1.1 copy-start.3
  18.1 3.8 copy-start.10
  18.1 5.2 copy-start.9
  19.5 128.3 %all-gather.6.cloned.1.call-start = ((), (), s32[]{:S(2)}) async-start(), calls=%async_computation.1 | async-start | bytes 6684672 | tf_op jit(solution)/shard_map/all_gather | solution.py:64
  20.3 238.6 %all-gather.12.cloned.1.call-start = ((), (), s32[]{:S(2)}) async-start(), calls=%async_computation.4 | async-start | bytes 6684672 | tf_op jit(solution)/shard_map/all_gather | solution.py:113
  21.0 803.8 %reduce-scatter.4.cloned.1.call-start = ((), (), s32[]{:S(2)}) async-start(), calls=%async_computation.5 | async-start | bytes 4227072
  154.4 22.5 %copy-start.4 = (bf16[192,1024]{1,0:T(8,128)(2,1)S(1)}, bf16[192,1024]{1,0:T(8,128)(2,1)}, u32[]{:S(2)}) copy-start(bf16[192,1024]{1,0:T(8,128)(2,1)} %param.15) | copy-start | bytes 1179652
  186.1 727.7 %all-gather.10.cloned.1.call-start = ((), (), s32[]{:S(2)}) async-start(), calls=%async_computation.3 | async-start | bytes 6684672 | tf_op jit(solution)/shard_map/all_gather | solution.py:114
  188.2 2.4 copy-start.6
  195.5 61.0 %copy-start.2 = (bf16[192,1024]{1,0:T(8,128)(2,1)S(1)}, bf16[192,1024]{1,0:T(8,128)(2,1)}, u32[]{:S(2)}) copy-start(bf16[192,1024]{1,0:T(8,128)(2,1)} %param.11) | copy-start | bytes 1179652
  985.4 2.6 copy-start.7
  985.4 2.6 copy-start.8
  987.9 7.5 copy-start.5
  988.0 8.6 copy-start.1
Sparse Core Ops, SparseCore 0:
  19.6 65.2 all-gather.7
  87.0 60.7 all-gather.5
  149.9 60.8 all-gather.11
  213.0 611.7 reduce-scatter.3
  827.0 86.6 all-gather.9
where the time goes:
time: 1010 us; the launch traced here: 1000 us
  waiting for transfers between devices  703 us (70%)
  matrix products  167 us (17%)
  blocking collectives  62.2 us (6%)
  local copies, waits for them, and re-layouts  49.4 us (5%)
  between operations  14.7 us (1%)
    unnamed x6, waiting for transfers between devices  561 us
    all_gather x1, waiting for transfers between devices, on_device(): piece_grad = lax.all_gather(grad_mixed, 'ctx', axis=0, tiled=True)  87.1 us
    all_gather x1, blocking collectives, on_device(): lax.all_gather(history, 'ctx', axis=0, tiled=True)  62.2 us
    all_gather x1, waiting for transfers between devices, on_device(): lax.all_gather(own_keys, 'ctx', axis=0, tiled=True)  55.4 us
    dot_general x8, matrix products, query_head(): return jnp.dot(grad_scores, one_k, preferred_element_type=jnp.float32)  34.5 us
    transpose x6, local copies, waits for them, and re-layouts, head_major(): matrix.reshape(matrix.shape[0], HEADS, matrix.shape[1] // HEADS)  30.2 us
    dot_general x8, matrix products, key_head(): key_part = jnp.dot(grad_scores.T, one_q, preferred_element_type=jnp.float32)  28.8 us
    dot_general x8, matrix products, query_head(): jnp.dot(one_q, one_k.T, preferred_element_type=jnp.float32) * score_scale  24.4 us
  transfers between devices with their start and end apart: 5, of which 3 were waited for; matrix products, arithmetic and copies ran while one was open for 13% of the time, Pallas kernels for 0%

commit v1 on v0

--- a/solution.py
+++ b/solution.py
@@ -110,8 +110,11 @@
     grad_queries = row_major(lax.map(query_head, (query_h, keys_h, values_h, grad_h)))
     own_keys_h = head_major(own_keys)
     own_values_h = head_major(own_values)
-    piece_q = lax.all_gather(queries, "ctx", axis=0, tiled=True)
-    piece_grad = lax.all_gather(grad_mixed, "ctx", axis=0, tiled=True)
+    piece_q, piece_grad = jnp.split(
+        lax.all_gather(jnp.concatenate([queries, grad_mixed], axis=1), "ctx", axis=0, tiled=True),
+        [queries.shape[1]],
+        axis=1,
+    )
     piece_hist = lax.all_gather(history, "ctx", axis=0, tiled=True)
     row_count = piece_q.shape[0]
     piece_pos = place_of(jnp.arange(row_count, dtype=jnp.int32), own_rows, ctx_count)

time: 1010 us -> 1020 us (level)
  waiting for transfers between devices: 703 us -> 714 us
    all_gather x2 -> x1, waiting for transfers between devices: 87.1 us -> 116 us  [on_device(): lax.all_gather(jnp.concatenate([queries, grad_mixed], axis=1), 'ctx', axi...]
    unnamed x6 -> x5, waiting for transfers between devices: 561 us -> 541 us
    transpose x6 -> x4, local copies, waits for them, and re-layouts: 30.2 us -> 16 us  [head_major(): matrix.reshape(matrix.shape[0], HEADS, matrix.shape[1] // HEADS)]
  transfers between devices with their start and end apart: 5 -> 4, of which waited for: 3 -> 3; matrix products, arithmetic and copies ran while one was open for 13% -> 8% of each run, Pallas kernels for 0% -> 0%
where the time goes in v1:
time: 1020 us; the launch traced here: 1010 us
  waiting for transfers between devices  714 us (70%)
  matrix products  166 us (16%)
  blocking collectives  62.1 us (6%)
  local copies, waits for them, and re-layouts  49.1 us (5%)
  between operations  14.5 us (1%)
    unnamed x5, waiting for transfers between devices  541 us
    all_gather x1, waiting for transfers between devices, on_device(): lax.all_gather(jnp.concatenate([queries, grad_mixed], axis=1), 'ctx', axi...  116 us
    all_gather x1, blocking collectives, on_device(): lax.all_gather(history, 'ctx', axis=0, tiled=True)  62.1 us
    all_gather x1, waiting for transfers between devices, on_device(): lax.all_gather(own_keys, 'ctx', axis=0, tiled=True)  56.3 us
    dot_general x8, matrix products, query_head(): return jnp.dot(grad_scores, one_k, preferred_element_type=jnp.float32)  34.4 us
    dot_general x8, matrix products, key_head(): key_part = jnp.dot(grad_scores.T, one_q, preferred_element_type=jnp.float32)  28.8 us
    dot_general x8, matrix products, query_head(): jnp.dot(one_q, one_k.T, preferred_element_type=jnp.float32) * score_scale  24.3 us
    dot_general x8, matrix products, forward_head(): return jnp.dot(weights, one_v, preferred_element_type=jnp.float32)  21.8 us
  transfers between devices with their start and end apart: 4, of which 3 were waited for; matrix products, arithmetic and copies ran while one was open for 8% of the time, Pallas kernels for 0%

profile of v1, /device:TPU:1, one launch (start us, length us, event | category | flops | bytes accessed | tf_op | source)
XLA Modules:
  0.0 1013.6 jit_solution(7244850895848542016)
XLA Ops:
  9.8 7.2 multiply_convert_fusion
  22.6 62.1 %all-reduce = s32[3072]{0:T(1024)S(1)} all-reduce(s32[3072]{0:T(1024)S(1)} %dynamic-update-slice), channel_id=2, replica_groups=mesh['dp'=8,'ctx'=16] {'ctx'}, use_global_device_ids=true, to_apply=%add | all-reduce | flops 3072 | bytes 24576 | tf_op jit(solution)/shard_map/all_gather | solution.py:66
  84.8 6.5 bitcast_bitcast_fusion.2
  91.3 56.3 %all-gather.5.cloned.1.call-done = bf16[3072,1024]{1,0:T(8,128)(2,1)} async-done(((bf16[192,1024]{1,0:T(8,128)(2,1)}), bf16[3072,1024]{1,0:T(8,128)(2,1)}) %all-gather.5.cloned.1.call-update) | async-done | bytes 6291472 | tf_op jit(solution)/shard_map/all_gather | solution.py:64
  147.5 6.5 bitcast_bitcast_fusion.3
  154.1 21.9 %while.35 = (s32[]{:T(128)}, f32[8,192,128]{2,1,0:T(8,128)S(1)}, bf16[8,192,128]{2,1,0:T(8,128)(2,1)}, bf16[8,3072,128]{2,1,0:T(8,128)(2,1)}, bf16[8,3072,128]{2...) while((s32[]{:T(128)}, f32[8,192,128]{2,1,0:T(8,128)S(1)}, ...), condition=%wide.region_3.4_spmd.clone, body=%wide.region_2.3_spmd.clone.sunk | while | flops 307888128 | bytes 1749093 | solution.py:82
  176.5 3.8 convolution_bitcast_fusion
  180.2 5.3 copy.34
  194.9 58.7 %while.37 = (s32[]{:T(128)}, f32[8,192,128]{2,1,0:T(8,128)}, bf16[8,192,128]{2,1,0:T(8,128)(2,1)}, bf16[8,3072,128]{2,1,0:T(8,128)(2,1)}, bf16[8,192,128]{2,1,0:...) while((s32[]{:T(128)}, f32[8,192,128]{2,1,0:T(8,128)}, ...), condition=%wide.region_11.12_spmd.clone, body=%wide.region_10.11_spmd.clone.sunk | while | flops 461832192 | bytes 7303789 | solution.py:110
  198.0 4.3 fusion.200
  205.3 4.3 fusion.200
  212.6 4.3 fusion.200
  219.9 4.3 fusion.200
  227.3 4.3 fusion.200
  234.6 4.3 fusion.200
  242.0 4.3 fusion.200
  249.3 4.3 fusion.200
  258.1 540.5 %reduce-scatter.4.cloned.1.call-done = f32[8,1024]{1,0:T(8,128)} async-done(((f32[1024,1024]{1,0:T(8,128)}), f32[8,1024]{1,0:T(8,128)}) %reduce-scatter.4.cloned.1.call-update) | async-done | bytes 32784
  800.4 116.3 %all-gather.9.cloned.1.call-done = bf16[3072,2048]{1,0:T(8,128)(2,1)} async-done(((bf16[192,2048]{1,0:T(8,128)(2,1)}), bf16[3072,2048]{1,0:T(8,128)(2,1)}) %all-gather.9.cloned.1.call-update) | async-done | bytes 12582928 | tf_op jit(solution)/shard_map/all_gather | solution.py:114
  916.7 6.5 slice_bitcast_fusion
  923.2 3.8 copy.72
  927.0 3.8 copy.73
  932.8 63.1 %while.36 = (s32[]{:T(128)}, f32[8,192,128]{2,1,0:T(8,128)}, f32[8,192,128]{2,1,0:T(8,128)}, bf16[8,3072,128]{2,1,0:T(8,128)(2,1)}, bf16[8,192,128]{2,1,0:T(8,12...) while((s32[]{:T(128)}, f32[8,192,128]{2,1,0:T(8,128)}, ...), condition=%wide.region_9.10_spmd.clone, body=%wide.region_8.9_spmd.clone.sunk | while | flops 618135552 | bytes 10574965 | solution.py:137
  998.5 7.4 fusion.148
  (106 shorter events, 138.4 us)
Async XLA Ops:
  7.2 178.5 %copy-start = (bf16[1024,1024]{1,0:T(8,128)(2,1)S(1)}, bf16[1024,1024]{1,0:T(8,128)(2,1)}, u32[]{:S(2)}) copy-start(bf16[1024,1024]{1,0:T(8,128)(2,1)} %param.14) | copy-start | bytes 6291460
  7.2 77.6 %all-gather.7.cloned.1.call-start = ((), (), s32[]{:S(2)}) async-start(), calls=%async_computation.2 | async-start | bytes 6684672 | tf_op jit(solution)/shard_map/all_gather | solution.py:65
  16.9 1.1 copy-start.3
  18.1 3.1 copy-start.10
  18.1 4.2 copy-start.9
  19.5 128.0 %all-gather.5.cloned.1.call-start = ((), (), s32[]{:S(2)}) async-start(), calls=%async_computation.1 | async-start | bytes 6684672 | tf_op jit(solution)/shard_map/all_gather | solution.py:64
  20.3 778.4 %reduce-scatter.4.cloned.1.call-start = ((), (), s32[]{:S(2)}) async-start(), calls=%async_computation.4 | async-start | bytes 4227072
  154.1 22.3 %copy-start.4 = (bf16[192,1024]{1,0:T(8,128)(2,1)S(1)}, bf16[192,1024]{1,0:T(8,128)(2,1)}, u32[]{:S(2)}) copy-start(bf16[192,1024]{1,0:T(8,128)(2,1)} %param.15) | copy-start | bytes 1179652
  185.6 731.1 %all-gather.9.cloned.1.call-start = ((), (), s32[]{:S(2)}) async-start(), calls=%async_computation.3 | async-start | bytes 13369344 | tf_op jit(solution)/shard_map/all_gather | solution.py:114
  187.7 2.3 copy-start.6
  194.9 60.8 %copy-start.2 = (bf16[192,1024]{1,0:T(8,128)(2,1)S(1)}, bf16[192,1024]{1,0:T(8,128)(2,1)}, u32[]{:S(2)}) copy-start(bf16[192,1024]{1,0:T(8,128)(2,1)} %param.11) | copy-start | bytes 1179652
  995.9 2.6 copy-start.7
  995.9 2.6 copy-start.8
  998.5 7.5 copy-start.5
  998.5 8.6 copy-start.1
Sparse Core Ops, SparseCore 0:
  19.6 64.8 all-gather.6
  86.7 60.8 all-gather.4
  185.7 612.8 reduce-scatter.3
  800.8 115.8 all-gather.8
